TPU v7x, 32 devices: a whole 2x2x4 slice. The times are simulated.
32 devices in a mesh: cfg: 2 (over core), row: 4 (over z), col: 4 (over y, x).
Axes of the slice: x: 2, y: 2, z: 4, core: 2. Of those that a mesh axis runs over, the one named last changes fastest.
Arguments:
- img_tokens: bfloat16 [2, 4, 1024, 3072], P('cfg', 'col', None, 'row'), may hold values from -6 to 6
- txt_tokens: bfloat16 [2, 4, 512, 3072], P('cfg', 'col', None, 'row'), may hold values from -6 to 6
- img_mod: bfloat16 [2, 4, 2, 3072], P('cfg', 'col', None, 'row'), may hold values from -3 to 3
- txt_mod: bfloat16 [2, 4, 2, 3072], P('cfg', 'col', None, 'row'), may hold values from -3 to 3
- img_gate: bfloat16 [2, 4, 3072], P('cfg', 'col', 'row'), may hold values from -16 to 16
- txt_len: int32 [2, 4], P('cfg', 'col'), may hold values from 128 to 512, as said below
- img_qkv_weight: bfloat16 [3072, 3, 3072], P('col', None, 'row'), may hold values from -0.109375 to 0.109375
- txt_kv_weight: bfloat16 [3072, 2, 3072], P('col', None, 'row'), may hold values from -0.109375 to 0.109375
- out_weight: bfloat16 [3072, 3072], P('row', 'col'), may hold values from -0.109375 to 0.109375
- final_weight: bfloat16 [3072, 64], P('row'), may hold values from -0.109375 to 0.109375
- latent: float32 [4, 1024, 64], P('col', ('cfg', 'row')), may hold values from -6 to 6
- sigmas: float32 [5], replicated, may hold values from 0 to 2, as said below
- step_index: int32 [1], replicated, may hold values from 0 to 3
- guidance: float32 [1], replicated, may hold values from 1.5 to 5
Outputs:
- img_out: bfloat16 [2, 4, 1024, 3072], P('cfg', 'col', None, 'row')
- latent_next: float32 [4, 1024, 64], P('col', ('cfg', 'row'))
Inputs may be any that keep to these rules, and one draw needn't show every extreme that they name: `txt_len`: in each half some prompt has all 512 text slots live and some other prompt exactly 128. `sigmas`: falls strictly along the table.
All inputs are finite; a program needn't handle non-finite values.
Results may differ from a plain program's by a relative error of at most 0.015.
Values may be sent and summed in bfloat16 or wider, within the bound.
A program may use at most 128 MiB of HBM per device.

v0:
```python
import math

import jax
import jax.numpy as jnp
from jax import lax
from jax.sharding import PartitionSpec as P

HD = 128


def modulate(tokens, shift_scale):
    values = tokens.astype(jnp.float32)
    centre = values - jnp.mean(values, -1, keepdims=True)
    spread = jnp.mean(centre * centre, -1, keepdims=True)
    normed = centre * lax.rsqrt(spread + 1e-06)
    scaled = normed * (1.0 + shift_scale[..., 1:2, :].astype(jnp.float32))
    return (scaled + shift_scale[..., 0:1, :].astype(jnp.float32)).astype(jnp.bfloat16)


def rms_norm(values):
    return values * lax.rsqrt(jnp.mean(values * values, -1, keepdims=True) + 1e-06)


def add_rows(piece, ready):
    return jnp.dot(ready, piece.reshape(piece.shape[0], -1), preferred_element_type=jnp.float32)


def shards(
    img_tokens,
    txt_tokens,
    img_mod,
    txt_mod,
    img_gate,
    txt_len,
    img_qkv_weight,
    txt_kv_weight,
    out_weight,
    final_weight,
    latent,
    sigmas,
    step_index,
    guidance,
):
    img_whole, txt_whole, img_shift, txt_shift = (
        lax.all_gather(img_tokens, "row", axis=3, tiled=True),
        lax.all_gather(txt_tokens, "row", axis=3, tiled=True),
        lax.all_gather(img_mod, "row", axis=3, tiled=True),
        lax.all_gather(txt_mod, "row", axis=3, tiled=True),
    )
    prompts = img_tokens.shape[1]
    images = img_tokens.shape[2]
    text_slots = txt_tokens.shape[2]
    local_width = img_qkv_weight.shape[2]
    heads_here = local_width // HD
    img_ready = modulate(img_whole[0], img_shift[0]).reshape(prompts * images, -1)
    txt_ready = modulate(txt_whole[0], txt_shift[0]).reshape(prompts * text_slots, -1)
    img_proj = add_rows(lax.all_gather(img_qkv_weight, "col", axis=0, tiled=True), img_ready)
    txt_proj = add_rows(lax.all_gather(txt_kv_weight, "col", axis=0, tiled=True), txt_ready)
    img_proj = img_proj.reshape(prompts, images, 3, heads_here, HD)
    txt_proj = txt_proj.reshape(prompts, text_slots, 2, heads_here, HD)
    queries = rms_norm(img_proj[:, :, 0]).astype(jnp.bfloat16)
    key_rows = jnp.concatenate(
        [rms_norm(txt_proj[:, :, 0]), rms_norm(img_proj[:, :, 1])], 1
    ).astype(jnp.bfloat16)
    value_rows = jnp.concatenate([txt_proj[:, :, 1], img_proj[:, :, 2]], 1).astype(jnp.bfloat16)
    positions = jnp.arange(text_slots + images, dtype=jnp.int32)
    scores = jnp.einsum(
        "qhe,khe->hqk", queries[0], key_rows[0], preferred_element_type=jnp.float32
    ) / math.sqrt(HD)
    usable = (positions < txt_len[0, 0]) | (positions >= text_slots)
    weights = jnp.where(usable, jnp.exp(scores), 0.0)
    chances = (weights / jnp.sum(weights, -1, keepdims=True)).astype(jnp.bfloat16)
    mixed = jnp.einsum("hqk,khe->qhe", chances, value_rows[0], preferred_element_type=jnp.float32)
    outputs = mixed.reshape(images, local_width).astype(jnp.bfloat16)
    head_terms = jnp.dot(
        outputs,
        lax.all_gather(out_weight, "col", axis=1, tiled=True),
        preferred_element_type=jnp.float32,
    )
    projected = (
        lax.psum_scatter(head_terms.astype(jnp.bfloat16), "row", scatter_dimension=1, tiled=True)
        .astype(jnp.float32)
        .reshape(prompts, images, local_width)
    )
    gating = img_gate[0][:, None, :].astype(jnp.float32)
    img_out = (img_tokens[0].astype(jnp.float32) + gating * projected).astype(jnp.bfloat16)
    velocity = jnp.dot(
        img_out.reshape(prompts * images, local_width),
        final_weight,
        preferred_element_type=jnp.float32,
    )
    velocity = velocity.reshape(prompts, images, -1)
    strength = guidance[0]
    share = jnp.where(lax.axis_index("cfg") == 1, strength, 1.0 - strength)
    weighted = velocity * share
    halved = lax.psum_scatter(weighted.astype(jnp.bfloat16), "cfg", scatter_dimension=1, tiled=True)
    guided = lax.psum_scatter(halved, "row", scatter_dimension=1, tiled=True).astype(jnp.float32)
    position_now = step_index[0]
    step_size = sigmas[position_now + 1] - sigmas[position_now]
    return (img_out[None], latent + step_size * guided)


def solution(mesh):
    return jax.shard_map(
        shards,
        mesh=mesh,
        in_specs=(
            P("cfg", "col", None, "row"),
            P("cfg", "col", None, "row"),
            P("cfg", "col", None, "row"),
            P("cfg", "col", None, "row"),
            P("cfg", "col", "row"),
            P("cfg", "col"),
            P("col", None, "row"),
            P("col", None, "row"),
            P("row", "col"),
            P("row", None),
            P("col", ("cfg", "row"), None),
            P(),
            P(),
            P(),
        ),
        out_specs=(P("cfg", "col", None, "row"), P("col", ("cfg", "row"), None)),
        check_vma=False,
    )
```

profile of v0, /device:TPU:0, one launch (start us, length us, event | category | flops | bytes accessed | tf_op | source)
XLA Modules:
  0.0 648.4 jit_solution(333922999272282261)
XLA Ops:
  7.2 0.7 all-gather.6.cloned.1.call-update
  8.0 0.7 all-gather.10.cloned.1.call-update
  8.7 0.7 all-gather.8.cloned.1.call-update
  9.5 6.0 copy.22
  16.2 14.9 %all_gather.25 = bf16[1,1,2,3072]{3,2,1,0:T(2,128)(2,1)S(1)} all-gather(bf16[1,1,2,768]{3,2,1,0:T(2,128)(2,1)S(1)} %copy-done.8), channel_id=1, replica_groups=mesh['cfg'=2,'row'=4,'col'=4] {'row'}, dimensions={3}, use_global_device_ids=true | all-gather | bytes 15360 | tf_op jit(solution)/shard_map/all_gather | solution.py:47
  31.1 13.3 %all_gather.22 = bf16[1,1,2,3072]{3,2,1,0:T(2,128)(2,1)S(1)} all-gather(bf16[1,1,2,768]{3,2,1,0:T(2,128)(2,1)S(1)} %copy-done.9), channel_id=1, replica_groups=mesh['cfg'=2,'row'=4,'col'=4] {'row'}, dimensions={3}, use_global_device_ids=true | all-gather | bytes 15360 | tf_op jit(solution)/shard_map/all_gather | solution.py:48
  45.1 30.9 %all-gather.6.cloned.1.call-done = bf16[1,1,512,3072]{3,2,1,0:T(8,128)(2,1)} async-done(((bf16[1,1,512,768]{3,2,1,0:T(8,128)(2,1)}), bf16[1,1,512,3072]{3,2,1,0:T(8,128)(2,1)}) %all-gather.6.cloned.1.call-update) | async-done | bytes 3145744 | tf_op jit(solution)/shard_map/all_gather | solution.py:46
  76.0 2.5 convert_reduce_fusion.1
  78.8 1.0 fusion.15
  79.8 111.9 %all-gather.10.cloned.1.call-done = bf16[1,1,1024,3072]{3,2,1,0:T(8,128)(2,1)} async-done(((bf16[1,1,1024,768]{3,2,1,0:T(8,128)(2,1)}), bf16[1,1,1024,3072]{3,2,1,0:T(8,128)(2,1)}) %all-gather.10.cloned.1.call-update) | async-done | bytes 6291472 | tf_op jit(solution)/shard_map/all_gather | solution.py:45
  191.7 3.8 convert_reduce_fusion
  195.5 0.8 copy-done.1
  196.3 1.8 fusion.8
  198.0 90.0 %all-gather.8.cloned.1.call-done = bf16[3072,2,768]{2,1,0:T(2,128)(2,1)} async-done(((bf16[768,2,768]{2,1,0:T(2,128)(2,1)}), bf16[3072,2,768]{2,1,0:T(2,128)(2,1)}) %all-gather.8.cloned.1.call-update) | async-done | bytes 9437200 | tf_op jit(solution)/shard_map/all_gather | solution.py:58
  288.1 24.2 %copy.27 = bf16[3072,2,768]{0,2,1:T(8,128)(2,1)} copy(bf16[3072,2,768]{2,1,0:T(2,128)(2,1)} %all-gather.8.cloned.1.call-done) | data formatting | bytes 18874368 | tf_op jit(solution)/shard_map/reshape | solution.py:25
  312.2 8.4 %fusion.43 = f32[1,512,2,6,128]{4,1,3,2,0:T(8,128)S(1)} fusion(bf16[2,6,128,3072]{3,2,1,0:T(8,128)(2,1)} %bitcast.110, bf16[1,1,512,3072]{3,2,1,0:T(8,128)(2,1)S(1)} %copy-done.3, f32[3072]{0:T(1024)S(1)} %bitcast.120, f32[3072]{0:T(1024)S(1)} %bitcast.119, f32[512]{0:T(512)S(1)} %add_rsqrt_fusion.4, f32[512]{0:T(512)S(1)} %broadcast_multiply_fusion.1), kind=kOutput, calls=%fused_computation.54 | convolution fusion | flops 4841275392 | bytes 15757312 | tf_op jit(solution)/shard_map/dot_general | solution.py:25
  321.7 103.7 %all-gather.12.cloned.1.call-done = bf16[3072,3,768]{0,2,1:T(8,128)(2,1)} async-done(((bf16[768,3,768]{0,2,1:T(8,128)(2,1)}), bf16[3072,3,768]{0,2,1:T(8,128)(2,1)}) %all-gather.12.cloned.1.call-update) | async-done | bytes 14155792 | tf_op jit(solution)/shard_map/all_gather | solution.py:57
  425.4 21.6 %fusion.23 = f32[1,1024,3,6,128]{4,1,3,2,0:T(8,128)S(1)} fusion(bf16[3,6,128,3072]{3,2,1,0:T(8,128)(2,1)} %bitcast.121, bf16[1,1,1024,3072]{3,2,1,0:T(8,128)(2,1)} %all-gather.10.cloned.1.call-done, f32[3072]{0:T(1024)S(1)} %bitcast.118, f32[3072]{0:T(1024)S(1)} %bitcast.117, f32[1024]{0:T(1024)S(1)} %add_rsqrt_fusion.3, f32[1024]{0:T(1024)S(1)} %broadcast_multiply_fusion), kind=kOutput, calls=%fused_computation.31 | convolution fusion | flops 14514388992 | bytes 29917184 | tf_op jit(solution)/shard_map/dot_general | solution.py:25
  447.0 1.7 multiply_reduce_fusion.1
  448.7 1.0 fusion.30
  449.7 0.9 copy-done.2
  450.6 18.0 %fusion = (f32[6,1024]{1,0:T(8,128)S(1)}, f32[6,1024,1536]{2,1,0:T(8,128)}) fusion(pred[1536]{0:T(1024)(128)(4,1)S(1)} %fusion.60, bf16[1024,6,128]{2,0,1:T(8,128)(2,1)S(1)} %fusion.30, bf16[512,6,128]{2,0,1:T(8,128)(2,1)S(1)} %fusion.51, f32[1,1024,3,6,128]{4,1,3,2,0:T(8,128)} %copy-done.2, f32[1024,6]{0,1:T(8,128)S(1)} %get-tuple-element.9), kind=kOutput, calls=%fused_computation.2 | convolution fusion | flops 2450515968 | bytes 43304448 | tf_op jit(solution)/shard_map/qhe,khe->hqk/dot_general | solution.py:67
  468.6 2.1 fusion.50
  470.7 15.2 %fusion.46 = bf16[6,128,1024]{2,1,0:T(8,128)(2,1)S(1)} fusion(f32[6,1024,1536]{2,1,0:T(8,128)} %get-tuple-element.7, f32[6,1024]{1,0:T(8,128)S(1)} %get-tuple-element.6, pred[1536]{0:T(1024)(128)(4,1)S(1)} %fusion.60, bf16[1024,6,128]{2,0,1:T(8,128)(2,1)S(1)} %fusion.50, bf16[512,6,128]{2,0,1:T(8,128)(2,1)S(1)} %fusion.55), kind=kOutput, calls=%fused_computation.55 | convolution fusion | flops 2459172864 | bytes 41707008 | tf_op jit(solution)/shard_map/hqk,khe->qhe/dot_general | solution.py:73
  486.0 9.4 %convolution_convert_fusion = bf16[1024,3072]{1,0:T(8,128)(2,1)} fusion(bf16[1024,768]{0,1:T(8,128)(2,1)S(1)} %bitcast.122, bf16[768,3072]{1,0:T(8,128)(2,1)} %all-gather.14.cloned.1.call-done), kind=kOutput, calls=%fused_computation.30 | convolution fusion | flops 4834983936 | bytes 12582912 | tf_op jit(solution)/shard_map/dot_general | solution.py:75
  496.2 110.2 %reduce-scatter.6.cloned.1.call-done = bf16[1024,768]{1,0:T(8,128)(2,1)} async-done(((bf16[1024,3072]{1,0:T(8,128)(2,1)}), bf16[1024,768]{1,0:T(8,128)(2,1)}) %reduce-scatter.6.cloned.1.call-update) | async-done | bytes 1572880 | tf_op jit(solution)/shard_map/reduce_scatter | solution.py:81
  606.4 2.8 fusion.54
  611.8 5.6 reduce-scatter.8.cloned.1.call-done
  617.5 1.0 copy.28
  619.2 1.6 fusion.57
  620.8 19.3 %reduce-scatter.10.cloned.1.call-done = bf16[128,64]{1,0:T(8,128)(2,1)} async-done(((bf16[512,64]{1,0:T(8,128)(2,1)}), bf16[128,64]{1,0:T(8,128)(2,1)}) %reduce-scatter.10.cloned.1.call-update) | async-done | bytes 16400
  640.1 0.8 reshape_bitcast_fusion
  (53 shorter events, 4.4 us)
Async XLA Ops:
  7.2 599.3 %copy-start = (bf16[768,64]{0,1:T(8,128)(2,1)S(1)}, bf16[768,64]{0,1:T(8,128)(2,1)}, u32[]{:S(2)}) copy-start(bf16[768,64]{0,1:T(8,128)(2,1)} %param.23) | copy-start | bytes 294916
  7.2 68.8 %all-gather.6.cloned.1.call-start = ((), (), s32[]{:S(2)}) async-start(), calls=%async_computation.3 | async-start | bytes 3932160 | tf_op jit(solution)/shard_map/all_gather | solution.py:46
  7.9 183.7 %all-gather.10.cloned.1.call-start = ((), (), s32[]{:S(2)}) async-start(), calls=%async_computation.5 | async-start | bytes 7864320 | tf_op jit(solution)/shard_map/all_gather | solution.py:45
  8.7 279.4 %all-gather.8.cloned.1.call-start = ((), (), s32[]{:S(2)}) async-start(), calls=%async_computation.4 | async-start | bytes 11796480 | tf_op jit(solution)/shard_map/all_gather | solution.py:58
  9.4 6.7 %copy-start.8 = (bf16[1,1,2,768]{3,2,1,0:T(2,128)(2,1)S(1)}, bf16[1,1,2,768]{3,2,1,0:T(2,128)(2,1)}, u32[]{:S(2)}) copy-start(bf16[1,1,2,768]{3,2,1,0:T(2,128)(2,1)} %param.16) | copy-start | bytes 9220
  9.4 21.7 %copy-start.9 = (bf16[1,1,2,768]{3,2,1,0:T(2,128)(2,1)S(1)}, bf16[1,1,2,768]{3,2,1,0:T(2,128)(2,1)}, u32[]{:S(2)}) copy-start(bf16[1,1,2,768]{3,2,1,0:T(2,128)(2,1)} %param.17) | copy-start | bytes 9220
  9.4 416.0 %all-gather.12.cloned.1.call-start = ((), (), s32[]{:S(2)}) async-start(), calls=%async_computation.6 | async-start | bytes 17694720 | tf_op jit(solution)/shard_map/all_gather | solution.py:57
  15.5 470.5 %all-gather.14.cloned.1.call-start = ((), (), s32[]{:S(2)}) async-start(), calls=%async_computation.7 | async-start | bytes 5898240 | tf_op jit(solution)/shard_map/all_gather | solution.py:77
  16.1 590.3 %reduce-scatter.6.cloned.1.call-start = ((), (), s32[]{:S(2)}) async-start(), calls=%async_computation.8 | async-start | bytes 7864320 | tf_op jit(solution)/shard_map/reduce_scatter | solution.py:81
  76.0 2.8 copy-start.3
  191.7 4.6 copy-start.1
  447.0 3.6 copy-start.2
  495.3 0.8 copy-start.7
  495.3 111.1 %copy-start.4 = (bf16[1,1,1024,768]{3,2,1,0:T(8,128)(2,1)S(1)}, bf16[1,1,1024,768]{3,2,1,0:T(8,128)(2,1)}, u32[]{:S(2)}) copy-start(bf16[1,1,1024,768]{3,2,1,0:T(8,128)(2,1)} %param.14) | copy-start | bytes 4718596
  495.3 114.7 %copy-start.10 = (f32[5]{0:T(128)S(1)}, f32[5]{0:T(128)}, u32[]{:S(2)}) copy-start(f32[5]{0:T(128)} %param.25) | copy-start | bytes 64
  495.4 122.1 %reduce-scatter.8.cloned.1.call-start = ((), (), s32[]{:S(2)}) async-start(), calls=%async_computation.9 | async-start | bytes 196608 | tf_op jit(solution)/shard_map/reduce_scatter | solution.py:96
  496.2 144.8 %copy-start.6 = (f32[1,128,64]{1,2,0:T(8,128)S(1)}, f32[1,128,64]{1,2,0:T(8,128)}, u32[]{:S(2)}) copy-start(f32[1,128,64]{1,2,0:T(8,128)} %param.24) | copy-start | bytes 98308
  606.4 12.7 %copy-start.5 = (bf16[1024,768]{1,0:T(8,128)(2,1)S(1)}, bf16[1024,768]{1,0:T(8,128)(2,1)}, u32[]{:S(2)}) copy-start(bf16[1024,768]{1,0:T(8,128)(2,1)} %reduce-scatter.6.cloned.1.call-done) | copy-start | bytes 4718596
  609.3 30.8 %reduce-scatter.10.cloned.1.call-start = ((), (), s32[]{:S(2)}) async-start(), calls=%async_computation.10 | async-start | bytes 163840
Sparse Core Ops, SparseCore 0:
  9.6 66.3 all-gather.5
  77.5 114.0 all-gather.9
  193.5 94.5 all-gather.7
  289.8 135.6 all-gather.11
  427.1 57.0 all-gather.13
  495.5 110.9 reduce-scatter.5
  609.4 7.9 reduce-scatter.7
  619.7 20.3 reduce-scatter.9
where the time goes:
time: 650 us; the launch traced here: 648 us
  waiting for transfers between devices  474 us (73%)
  matrix products  75.4 us (12%)
  local copies, waits for them, and re-layouts  37.5 us (6%)
  blocking collectives  28.2 us (4%)
  between operations  17.7 us (3%)
  other arithmetic  15.1 us (2%)
    all_gather x1, waiting for transfers between devices, shards(): lax.all_gather(img_tokens, 'row', axis=3, tiled=True)  112 us
    reduce_scatter x1, waiting for transfers between devices, shards(): lax.psum_scatter(head_terms.astype(jnp.bfloat16), 'row', scatter_dimensio...  110 us
    all_gather x1, waiting for transfers between devices, shards(): lax.all_gather(img_qkv_weight, 'col', axis=0, tiled=True)  104 us
    all_gather x1, waiting for transfers between devices, shards(): lax.all_gather(txt_kv_weight, 'col', axis=0, tiled=True)  90 us
    all_gather x1, waiting for transfers between devices, shards(): lax.all_gather(txt_tokens, 'row', axis=3, tiled=True)  30.9 us
    dot_general x2, matrix products, add_rows(): jnp.dot(ready, piece.reshape(piece.shape[0], -1), preferred_element_type=...  30 us
    reshape x1, local copies, waits for them, and re-layouts, add_rows(): piece.reshape(piece.shape[0], -1)  24.2 us
    unnamed x9, waiting for transfers between devices  22 us
  transfers between devices with their start and end apart: 8, of which 7 were waited for; matrix products, arithmetic and copies ran while one was open for 17% of the time, Pallas kernels for 0%

commit v1 on v0

--- a/solution.py
+++ b/solution.py
@@ -1,8 +1,11 @@
+import functools
 import math
 
 import jax
 import jax.numpy as jnp
 from jax import lax
+from jax.experimental import pallas as pl
+from jax.experimental.pallas import tpu as pltpu
 from jax.sharding import PartitionSpec as P
 
 HD = 128
@@ -100,9 +103,520 @@
     return (img_out[None], latent + step_size * guided)
 
 
+ROWS = 256
+MESH = pl.DeviceIdType.MESH
+
+
+def layer_kernel(
+    scalars,
+    live_len,
+    img_hbm,
+    txt_hbm,
+    mods_hbm,
+    gate,
+    own_w,
+    final_w,
+    latent,
+    out,
+    latent_out,
+    tok,
+    weights,
+    mods,
+    ready,
+    q_buf,
+    k_buf,
+    v_buf,
+    from_up,
+    from_down,
+    mixed,
+    vel_send,
+    vel_recv,
+    up_send,
+    up_recv,
+    dn_send,
+    dn_recv,
+    w_send,
+    w_recv,
+    m_send,
+    m_recv,
+    sum_dn_send,
+    sum_dn_recv,
+    sum_up_send,
+    sum_up_recv,
+    v_send,
+    v_recv,
+    local,
+):
+    g, r, c = lax.axis_index("cfg"), lax.axis_index("row"), lax.axis_index("col")
+    n_row = 4
+    last = n_row - 1
+    images, width = img_hbm.shape
+    texts = txt_hbm.shape[0]
+    slots = images + texts
+    txt_chunks, img_chunks = texts // ROWS, images // ROWS
+    chunks = txt_chunks + img_chunks
+    heads = width // HD
+    half = width // 2
+    beside_x = c + 1 - 2 * lax.rem(c, 2)
+    beside_y = lax.rem(c + 2, 4)
+    across = lax.rem(beside_x + 2, 4)
+    sibling = (1 - g, r, c)
+    me = g * n_row + r
+
+    def peer(step):
+        other = lax.rem(me + step, 2 * n_row)
+        return other, (other // n_row, lax.rem(other, n_row), c)
+
+    barrier = pltpu.get_barrier_semaphore()
+    for step in range(1, 2 * n_row):
+        pl.semaphore_signal(barrier, inc=1, device_id=peer(step)[1], device_id_type=MESH)
+    for other in (beside_x, beside_y):
+        pl.semaphore_signal(barrier, inc=1, device_id=(g, r, other), device_id_type=MESH)
+    pl.semaphore_wait(barrier, 2 * n_row + 1)
+
+    def remote(a, b, send, recv, where):
+        return pltpu.make_async_remote_copy(
+            src_ref=a, dst_ref=b, send_sem=send, recv_sem=recv, device_id=where, device_id_type=MESH
+        )
+
+    def tok_at(source, j):
+        return tok.at[pl.ds(pl.multiple_of(source * slots + j * ROWS, ROWS), ROWS)]
+
+    def own_chunk(j):
+        if j < txt_chunks:
+            return txt_hbm.at[pl.ds(j * ROWS, ROWS)]
+        return img_hbm.at[pl.ds((j - txt_chunks) * ROWS, ROWS)]
+
+    def up_copy(hops, j, a=None):
+        b = tok_at(r - hops, j)
+        return remote(b if a is None else a, b, up_send.at[hops, j], up_recv.at[hops, j], (g, r + 1, c))
+
+    def dn_copy(hops, j, a=None):
+        b = tok_at(r + hops, j)
+        return remote(b if a is None else a, b, dn_send.at[hops, j], dn_recv.at[hops, j], (g, r - 1, c))
+
+    def w_at(p, source, core):
+        at = (p * 4 + source) * width + core * half
+        return weights.at[pl.ds(pl.multiple_of(at, half), half)]
+
+    def w_own(p):
+        return own_w.at[pl.ds(pl.multiple_of(p * width + g * half, half), half)]
+
+    def w_copy(p, i, a, b, where):
+        return remote(a, b, w_send.at[p, i], w_recv.at[p, i], where)
+
+    def to_x(p):
+        return w_copy(p, 0, w_own(p), w_at(p, c, g), (g, r, beside_x))
+
+    def to_y(p):
+        return w_copy(p, 1, w_own(p), w_at(p, c, g), (g, r, beside_y))
+
+    def onward(p):
+        source = jnp.where(g == 0, beside_x, beside_y)
+        target = jnp.where(g == 0, beside_y, beside_x)
+        return w_copy(p, 2, w_at(p, source, g), w_at(p, source, g), (g, r, target))
+
+    def share(p, i):
+        source = (beside_x, beside_y, across)[i]
+        return w_copy(p, 3 + i, w_at(p, source, g), w_at(p, source, g), sibling)
+
+    def mods_copy(step):
+        place = mods.at[pl.ds(pl.multiple_of(r * 16, 16), 16)]
+        return remote(mods_hbm, place, m_send.at[step - 1], m_recv.at[step - 1], (g, lax.rem(r + step, n_row), c))
+
+    for step in range(1, n_row):
+        mods_copy(step).start()
+    for j in range(chunks):
+
+        @pl.when(r < last)
+        def _():
+            up_copy(0, j, own_chunk(j)).start()
+
+        @pl.when(r > 0)
+        def _():
+            dn_copy(0, j, own_chunk(j)).start()
+
+        if j < 6:
+            to_x(j).start()
+            to_y(j).start()
+
+    locals_ = [
+        pltpu.make_async_copy(txt_hbm, tok.at[pl.ds(pl.multiple_of(r * slots, ROWS), texts)], local.at[0]),
+        pltpu.make_async_copy(img_hbm, tok.at[pl.ds(pl.multiple_of(r * slots + texts, ROWS), images)], local.at[1]),
+        pltpu.make_async_copy(mods_hbm, mods.at[pl.ds(pl.multiple_of(r * 16, 16), 16)], local.at[2]),
+    ]
+    for p in range(6):
+        locals_.append(
+            pltpu.make_async_copy(
+                own_w.at[pl.ds(p * width, width)],
+                weights.at[pl.ds(pl.multiple_of((p * 4 + c) * width, width), width)],
+                local.at[3 + p],
+            )
+        )
+    for copy in locals_:
+        copy.start()
+
+    def arrive(hops, j):
+        @pl.when(r > hops)
+        def _():
+            up_copy(hops, j).wait_recv()
+
+        @pl.when(r < last - hops)
+        def _():
+            dn_copy(hops, j).wait_recv()
+
+        if hops < n_row - 2:
+
+            @pl.when((r > hops) & (r < last))
+            def _():
+                up_copy(hops + 1, j).start()
+
+            @pl.when((r < last - hops) & (r > 0))
+            def _():
+                dn_copy(hops + 1, j).start()
+
+    @pl.loop(0, chunks)
+    def _(j):
+        arrive(0, j)
+        to_x(j).wait_recv()
+        to_y(j).wait_recv()
+        onward(j).start()
+        share(j, 0).start()
+        share(j, 1).start()
+
+    @pl.loop(0, chunks)
+    def _(j):
+        arrive(1, j)
+        onward(j).wait_recv()
+        share(j, 2).start()
+
+    for copy in locals_:
+        copy.wait()
+    for step in range(1, n_row):
+        mods_copy(step).wait_recv()
+
+    @pl.loop(0, chunks)
+    def _(j):
+        for i in range(3):
+            share(j, i).wait_recv()
+
+    def normalise(j, first):
+        @pl.loop(0, ROWS // 32)
+        def _(i):
+            parts = []
+            for s in range(n_row):
+                rows = pl.ds(pl.multiple_of(s * slots + j * ROWS + i * 32, 32), 32)
+                parts.append(tok[rows, :].astype(jnp.float32))
+            total = sum(jnp.sum(x, -1, keepdims=True) for x in parts)
+            mean = total / (n_row * width)
+            parts = [x - mean for x in parts]
+            spread = sum(jnp.sum(x * x, -1, keepdims=True) for x in parts) / (n_row * width)
+            scale = lax.rsqrt(spread + 1e-06)
+            for s in range(n_row):
+                table = mods[pl.ds(s * 16, 16), :].astype(jnp.float32)
+                value = parts[s] * scale * (1.0 + table[first + 1 : first + 2]) + table[first : first + 1]
+                ready[pl.ds(pl.multiple_of(i * 32, 32), 32), pl.ds(s * width, width)] = value.astype(jnp.bfloat16)
+
+    def project(p, put):
+        @pl.loop(0, heads // 2)
+        def _(t):
+            block = weights[pl.ds(p * 4 * width, 4 * width), pl.ds(pl.multiple_of(t * 2 * HD, 2 * HD), 2 * HD)]
+            y = jnp.dot(ready[...], block, preferred_element_type=jnp.float32)
+            put(2 * t, y[:, :HD])
+            put(2 * t + 1, y[:, HD:])
+
+    def put_keys(at):
+        def put(h, y):
+            k_buf[h, pl.ds(at, ROWS), :] = rms_norm(y).astype(jnp.bfloat16)
+
+        return put
+
+    def put_values(at, alive):
+        def put(h, y):
+            v_buf[h, pl.ds(at, ROWS), pl.ds(0, HD)] = (y if alive is None else y * alive).astype(jnp.bfloat16)
+            ones = jnp.ones((ROWS, HD), jnp.float32)
+            v_buf[h, pl.ds(at, ROWS), pl.ds(HD, HD)] = (ones if alive is None else ones * alive).astype(jnp.bfloat16)
+
+        return put
+
+    @pl.loop(0, txt_chunks)
+    def _(j):
+        arrive(2, j)
+        normalise(j, 2)
+        at = pl.multiple_of(j * ROWS, ROWS)
+        project(0, put_keys(at))
+        place = at + lax.broadcasted_iota(jnp.int32, (ROWS, HD), 0)
+        project(1, put_values(at, jnp.where(place < live_len[0], 1.0, 0.0)))
+
+    q_scale = math.log2(math.e) / math.sqrt(HD)
+
+    @pl.loop(0, img_chunks)
+    def _(i):
+        j = txt_chunks + i
+        arrive(2, j)
+        normalise(j, 0)
+        at = pl.multiple_of(j * ROWS, ROWS)
+        row = pl.multiple_of(i * ROWS, ROWS)
+        project(2, put_keys(at))
+        project(3, put_values(at, None))
+
+        def put_queries(h, y):
+            q_buf[h, pl.ds(row, ROWS), :] = (rms_norm(y) * q_scale).astype(jnp.bfloat16)
+
+        project(4, put_queries)
+
+    @pl.loop(0, 6)
+    def _(p):
+        to_x(p).wait_send()
+        to_y(p).wait_send()
+        onward(p).wait_send()
+        for i in range(3):
+            share(p, i).wait_send()
+
+    def term_at(d, b):
+        return pl.ds(pl.multiple_of(d * images + b * ROWS, ROWS), ROWS)
+
+    def down_copy(d, b):
+        return remote(
+            weights.at[term_at(d, b)], from_up.at[term_at(d, b)], sum_dn_send.at[d, b], sum_dn_recv.at[d, b], (g, r - 1, c)
+        )
+
+    def upward_copy(d, b):
+        return remote(
+            weights.at[term_at(d, b)],
+            from_down.at[term_at(d - 1, b)],
+            sum_up_send.at[d - 1, b],
+            sum_up_recv.at[d - 1, b],
+            (g, r + 1, c),
+        )
+
+    @pl.loop(0, img_chunks)
+    def _(b):
+        row = pl.multiple_of(b * ROWS, ROWS)
+        for h in range(heads):
+            scores = lax.dot_general(
+                q_buf[h, pl.ds(row, ROWS), :],
+                k_buf[h],
+                (((1,), (1,)), ((), ())),
+                preferred_element_type=jnp.float32,
+            )
+            chances = jnp.exp2(scores).astype(jnp.bfloat16)
+            y = jnp.dot(chances, v_buf[h], preferred_element_type=jnp.float32)
+            mixed[:, pl.ds(h * HD, HD)] = (y[:, :HD] / y[:, HD:]).astype(jnp.bfloat16)
+
+        @pl.loop(0, n_row)
+        def _(d):
+            block = weights[pl.ds(pl.multiple_of((20 + d) * width, width), width), :]
+            y = jnp.dot(mixed[...], block, preferred_element_type=jnp.float32)
+            weights[term_at(d, b), :] = y.astype(jnp.bfloat16)
+
+        for i in range(last):
+
+            @pl.when(r == last)
+            def _():
+                down_copy(i, b).start()
+
+            @pl.when(r == 0)
+            def _():
+                upward_copy(last - i, b).start()
+
+    strength = scalars[0]
+
+    def finish(b, projected):
+        own = tok[pl.ds(pl.multiple_of(r * slots + texts + b * ROWS, ROWS), ROWS), :].astype(jnp.float32)
+        result = (own + gate[...].astype(jnp.float32) * projected).astype(jnp.bfloat16)
+        rows = pl.ds(pl.multiple_of(b * ROWS, ROWS), ROWS)
+        out[rows, :] = result
+        velocity = jnp.dot(result, final_w[...], preferred_element_type=jnp.float32) * strength
+        vel_send[rows, :] = velocity.astype(jnp.bfloat16)
+
+    @pl.loop(0, img_chunks)
+    def _(b):
+        for i in range(last):
+            d = i
+
+            @pl.when((d < r) & (r < last))
+            def _():
+                down_copy(d, b).wait_recv()
+                total = weights[term_at(d, b), :].astype(jnp.float32) + from_up[term_at(d, b), :].astype(jnp.float32)
+                weights[term_at(d, b), :] = total.astype(jnp.bfloat16)
+                down_copy(d, b).start()
+
+            u = last - i
+
+            @pl.when((u > r) & (r > 0))
+            def _():
+                upward_copy(u, b).wait_recv()
+                total = weights[term_at(u, b), :].astype(jnp.float32) + from_down[term_at(u - 1, b), :].astype(jnp.float32)
+                weights[term_at(u, b), :] = total.astype(jnp.bfloat16)
+                upward_copy(u, b).start()
+
+        @pl.when(r < last)
+        def _():
+            down_copy(r, b).wait_recv()
+            total = weights[term_at(r, b), :].astype(jnp.float32) + from_up[term_at(r, b), :].astype(jnp.float32)
+
+            @pl.when(r == 0)
+            def _():
+                finish(b, total)
+
+            @pl.when(r > 0)
+            def _():
+                upward_copy(r, b).wait_recv()
+                finish(b, total + from_down[term_at(r - 1, b), :].astype(jnp.float32))
+
+        @pl.when(r == last)
+        def _():
+            upward_copy(r, b).wait_recv()
+            finish(
+                b, weights[term_at(r, b), :].astype(jnp.float32) + from_down[term_at(r - 1, b), :].astype(jnp.float32)
+            )
+
+    here = latent.shape[0]
+
+    def vel_copy(step):
+        other, where = peer(step)
+        return remote(
+            vel_send.at[pl.ds(pl.multiple_of(other * here, here), here)],
+            vel_recv.at[pl.ds(step * here, here)],
+            v_send.at[step - 1],
+            v_recv.at[step - 1],
+            where,
+        )
+
+    for step in range(1, 2 * n_row):
+        vel_copy(step).start()
+    guided = vel_send[pl.ds(pl.multiple_of(me * here, here), here), :].astype(jnp.float32)
+    for step in range(1, 2 * n_row):
+        vel_copy(step).wait_recv()
+        guided += vel_recv[pl.ds(step * here, here), :].astype(jnp.float32)
+    latent_out[...] = latent[...] + scalars[1] * guided[:, : latent.shape[1]]
+
+    for step in range(1, 2 * n_row):
+        vel_copy(step).wait_send()
+    for step in range(1, n_row):
+        mods_copy(step).wait_send()
+
+    @pl.loop(0, chunks)
+    def _(j):
+        for hops in range(last):
+
+            @pl.when((r >= hops) & (r < last))
+            def _():
+                up_copy(hops, j).wait_send()
+
+            @pl.when((r <= last - hops) & (r > 0))
+            def _():
+                dn_copy(hops, j).wait_send()
+
+    @pl.loop(0, img_chunks)
+    def _(b):
+        for i in range(last):
+
+            @pl.when(i < r)
+            def _():
+                down_copy(i, b).wait_send()
+
+            @pl.when(last - i > r)
+            def _():
+                upward_copy(last - i, b).wait_send()
+
+
+def fused(
+    img_tokens,
+    txt_tokens,
+    img_mod,
+    txt_mod,
+    img_gate,
+    txt_len,
+    img_qkv_weight,
+    txt_kv_weight,
+    out_weight,
+    final_weight,
+    latent,
+    sigmas,
+    step_index,
+    guidance,
+):
+    images, width = img_tokens.shape[2:]
+    texts = txt_tokens.shape[2]
+    slots = images + texts
+    heads = width // HD
+    chunks = slots // ROWS
+    blocks = images // ROWS
+    strength = guidance[0]
+    share = jnp.where(lax.axis_index("cfg") == 1, strength, 1.0 - strength)
+    now = step_index[0]
+    scalars = jnp.stack([share, sigmas[now + 1] - sigmas[now]])
+    txt_w = jnp.transpose(txt_kv_weight, (1, 0, 2)).reshape(2 * width, width)
+    img_w = jnp.transpose(img_qkv_weight, (1, 0, 2))
+    own_w = jnp.concatenate([txt_w, img_w[1], img_w[2], img_w[0], out_weight], 0)
+    mods = jnp.concatenate([img_mod[0, 0], txt_mod[0, 0], jnp.zeros((12, width), jnp.bfloat16)], 0)
+    final_w = jnp.pad(final_weight, ((0, 0), (0, HD - final_weight.shape[1])))
+    smem, vmem, anywhere = (
+        pl.BlockSpec(memory_space=pltpu.SMEM),
+        pl.BlockSpec(memory_space=pltpu.VMEM),
+        pl.BlockSpec(memory_space=pl.ANY),
+    )
+    dma = pltpu.SemaphoreType.DMA
+    here = latent.shape[1]
+    out, latent_out = pl.pallas_call(
+        layer_kernel,
+        out_shape=(
+            jax.ShapeDtypeStruct((images, width), jnp.bfloat16),
+            jax.ShapeDtypeStruct(latent.shape[1:], jnp.float32),
+        ),
+        in_specs=[smem, smem, anywhere, anywhere, anywhere, vmem, anywhere, vmem, vmem],
+        out_specs=(vmem, vmem),
+        scratch_shapes=[
+            pltpu.VMEM((4 * slots, width), jnp.bfloat16),
+            pltpu.VMEM((24 * width, width), jnp.bfloat16),
+            pltpu.VMEM((64, width), jnp.bfloat16),
+            pltpu.VMEM((ROWS, 4 * width), jnp.bfloat16),
+            pltpu.VMEM((heads, images, HD), jnp.bfloat16),
+            pltpu.VMEM((heads, slots, HD), jnp.bfloat16),
+            pltpu.VMEM((heads, slots, 2 * HD), jnp.bfloat16),
+            pltpu.VMEM((3 * images, width), jnp.bfloat16),
+            pltpu.VMEM((3 * images, width), jnp.bfloat16),
+            pltpu.VMEM((ROWS, width), jnp.bfloat16),
+            pltpu.VMEM((images, HD), jnp.bfloat16),
+            pltpu.VMEM((8 * here, HD), jnp.bfloat16),
+            dma((3, chunks)),
+            dma((3, chunks)),
+            dma((3, chunks)),
+            dma((3, chunks)),
+            dma((6, 6)),
+            dma((6, 6)),
+            dma((3,)),
+            dma((3,)),
+            dma((3, blocks)),
+            dma((3, blocks)),
+            dma((3, blocks)),
+            dma((3, blocks)),
+            dma((7,)),
+            dma((7,)),
+            dma((9,)),
+        ],
+        compiler_params=pltpu.CompilerParams(
+            collective_id=0, has_side_effects=True, vmem_limit_bytes=63 * 1024 * 1024
+        ),
+    )(
+        scalars,
+        txt_len[0],
+        img_tokens[0, 0],
+        txt_tokens[0, 0],
+        mods,
+        img_gate[0],
+        own_w,
+        final_w,
+        latent[0],
+    )
+    return out[None, None], latent_out[None]
+
+
 def solution(mesh):
     return jax.shard_map(
-        shards,
+        fused if mesh.shape["col"] == 4 and mesh.shape["row"] == 4 else shards,
         mesh=mesh,
         in_specs=(
             P("cfg", "col", None, "row"),

time: 650 us -> 333 us (0.51)
  waiting for transfers between devices: 474 us -> 0 us
  Pallas kernels: 0 us -> 310 us
  matrix products: 75.4 us -> 0 us
  blocking collectives: 28.2 us -> 0 us
  local copies, waits for them, and re-layouts: 37.5 us -> 17 us
  other arithmetic: 15.1 us -> 1.35 us
  between operations: 17.7 us -> 4.09 us
    all_gather x5 -> x0, waiting for transfers between devices: 336 us -> none  [the longest x1 112 us: shards(): lax.all_gather(img_tokens, 'row', axis=3, tiled=True)]
    pallas_call x0 -> x1, Pallas kernels: none -> 310 us  [fused(): pl.pallas_call(layer_kernel, out_shape=(jax.ShapeDtypeStruct((images, wid...]
    reduce_scatter x2 -> x0, waiting for transfers between devices: 116 us -> none  [the longest x1 110 us: shards(): lax.psum_scatter(head_terms.astype(jnp.bfloat16), 'row', scatter_dimensio...]
    dot_general x6 -> x0, matrix products: 75.4 us -> none  [the longest x2 30 us: add_rows(): jnp.dot(ready, piece.reshape(piece.shape[0], -1), preferred_element_type=...]
    all_gather x2 -> x0, blocking collectives: 28.2 us -> none  [the longest x1 14.9 us: shards(): lax.all_gather(img_mod, 'row', axis=3, tiled=True)]
    reshape x1 -> x0, local copies, waits for them, and re-layouts: 24.2 us -> none  [add_rows(): piece.reshape(piece.shape[0], -1)]
    unnamed x9 -> x0, waiting for transfers between devices: 22 us -> none
    reduce_sum x6 -> x0, other arithmetic: 11.2 us -> none  [the longest x2 6.35 us: modulate(): centre = values - jnp.mean(values, -1, keepdims=True)]
  transfers between devices with their start and end apart: 8 -> 0, of which waited for: 7 -> 0; matrix products, arithmetic and copies ran while one was open for 17% -> 0% of each run, Pallas kernels for 0% -> 0%
where the time goes in v1:
time: 333 us; the launch traced here: 332 us
  Pallas kernels  310 us (93%)
  local copies, waits for them, and re-layouts  17 us (5%)
  between operations  4.09 us (1%)
    pallas_call x1, Pallas kernels, fused(): pl.pallas_call(layer_kernel, out_shape=(jax.ShapeDtypeStruct((images, wid...  310 us
    unnamed x16, local copies, waits for them, and re-layouts  11.6 us

profile of v1, /device:TPU:0, one launch (start us, length us, event | category | flops | bytes accessed | tf_op | source)
XLA Modules:
  0.0 332.5 jit_solution(12010937505891081046)
XLA Ops:
  0.6 0.0 copy-start
  1.4 1.4 fusion.3
  4.8 0.7 pad_maximum_fusion.scalars
  5.5 2.0 copy.16
  7.5 0.0 copy-start.1
  7.5 0.0 copy-start.2
  7.5 0.0 copy-start.3
  7.5 1.6 constant_dynamic-update-slice_fusion.1
  9.1 0.0 copy-done
  9.1 1.1 fusion.2
  10.2 1.1 fusion.1
  11.3 1.1 fusion
  12.4 0.0 copy-done.1
  12.4 1.1 constant_dynamic-update-slice_fusion.own_w
  13.5 1.1 copy.17
  14.6 0.7 pad.4.final_w
  15.3 1.5 copy.18
  16.8 0.1 pad.7.clone
  16.9 0.0 copy-done.2
  16.9 0.0 copy-done.3
  16.9 0.7 maximum_maximum_fusion.mods_hbm
  18.2 310.1 %shard_map.149 = (bf16[1024,768]{1,0:T(8,128)(2,1)}, f32[128,64]{1,0:T(8,128)}) custom-call(f32[2]{0:T(128)} %pad_maximum_fusion.scalars, s32[1]{0:T(128)} %bitcast.27.live_len, bf16[1024,768]{1,0:T(8,128)(2,1)} %bitcast.40, bf16[512,768]{1,0:T(8,128)(2,1)} %bitcast.42, bf16[16,768]{1,0:T(8,128)(2,1)} %maximum_maximum_fusion.mods_hbm, ...), custom_call_target="tpu_custom_call" | custom-call | tf_op jit(solution)/shard_map/pallas_call | solution.py:563
  328.3 1.5 copy.19
  329.8 2.7 copy.28
  (1 shorter events, 0.0 us)
Async XLA Ops:
  0.6 8.4 %copy-start = (bf16[768,3,768]{2,0,1:T(8,128)(2,1)S(1)}, bf16[768,3,768]{2,0,1:T(8,128)(2,1)}, u32[]{:S(2)}) copy-start(bf16[768,3,768]{2,0,1:T(8,128)(2,1)} %param.20) | copy-start | bytes 10616836
  7.5 4.9 %copy-start.1 = (bf16[768,768]{1,0:T(8,128)(2,1)S(1)}, bf16[768,768]{1,0:T(8,128)(2,1)}, u32[]{:S(2)}) copy-start(bf16[768,768]{1,0:T(8,128)(2,1)} %param.22) | copy-start | bytes 3538948
  7.5 9.4 %copy-start.2 = (bf16[1,1,2,768]{3,2,1,0:T(2,128)(2,1)S(1)}, bf16[1,1,2,768]{3,2,1,0:T(2,128)(2,1)}, u32[]{:S(2)}) copy-start(bf16[1,1,2,768]{3,2,1,0:T(2,128)(2,1)} %param.17) | copy-start | bytes 9220
  7.5 9.4 %copy-start.3 = (bf16[1,1,2,768]{3,2,1,0:T(2,128)(2,1)S(1)}, bf16[1,1,2,768]{3,2,1,0:T(2,128)(2,1)}, u32[]{:S(2)}) copy-start(bf16[1,1,2,768]{3,2,1,0:T(2,128)(2,1)} %param.16) | copy-start | bytes 9220

commit v2 on v1

--- a/solution.py
+++ b/solution.py
@@ -104,6 +104,7 @@
 
 
 ROWS = 256
+AHEAD = 3
 MESH = pl.DeviceIdType.MESH
 
 
@@ -122,7 +123,6 @@
     tok,
     weights,
     mods,
-    ready,
     q_buf,
     k_buf,
     v_buf,
@@ -146,6 +146,7 @@
     v_send,
     v_recv,
     local,
+    go,
 ):
     g, r, c = lax.axis_index("cfg"), lax.axis_index("row"), lax.axis_index("col")
     n_row = 4
@@ -226,24 +227,26 @@
 
     for step in range(1, n_row):
         mods_copy(step).start()
-    for j in range(chunks):
-
-        @pl.when(r < last)
-        def _():
-            up_copy(0, j, own_chunk(j)).start()
-
-        @pl.when(r > 0)
-        def _():
-            dn_copy(0, j, own_chunk(j)).start()
-
-        if j < 6:
-            to_x(j).start()
-            to_y(j).start()
+    for p in range(AHEAD):
+        to_x(p).start()
+        to_y(p).start()
+
+    def start_own():
+        for j in range(chunks):
+
+            @pl.when(r < last)
+            def _():
+                up_copy(0, j, own_chunk(j)).start()
+
+            @pl.when(r > 0)
+            def _():
+                dn_copy(0, j, own_chunk(j)).start()
 
     locals_ = [
         pltpu.make_async_copy(txt_hbm, tok.at[pl.ds(pl.multiple_of(r * slots, ROWS), texts)], local.at[0]),
         pltpu.make_async_copy(img_hbm, tok.at[pl.ds(pl.multiple_of(r * slots + texts, ROWS), images)], local.at[1]),
         pltpu.make_async_copy(mods_hbm, mods.at[pl.ds(pl.multiple_of(r * 16, 16), 16)], local.at[2]),
+        pltpu.make_async_copy(img_hbm, out, local.at[9]),
     ]
     for p in range(6):
         locals_.append(
@@ -275,32 +278,77 @@
             def _():
                 dn_copy(hops + 1, j).start()
 
-    @pl.loop(0, chunks)
-    def _(j):
-        arrive(0, j)
-        to_x(j).wait_recv()
-        to_y(j).wait_recv()
-        onward(j).start()
-        share(j, 0).start()
-        share(j, 1).start()
-
-    @pl.loop(0, chunks)
-    def _(j):
-        arrive(1, j)
-        onward(j).wait_recv()
-        share(j, 2).start()
+    def arrivals(hops, low, high):
+        @pl.loop(low, high)
+        def _(j):
+            arrive(hops, j)
+
+    def direct(p):
+        to_x(p).wait_recv()
+        to_y(p).wait_recv()
+        if p + AHEAD < 6:
+            to_x(p + AHEAD).start()
+            to_y(p + AHEAD).start()
+        onward(p).start()
+        share(p, 0).start()
+        share(p, 1).start()
+
+    def diagonal(p):
+        onward(p).wait_recv()
+        share(p, 2).start()
+
+    def have(p):
+        for i in range(3):
+            share(p, i).wait_recv()
+
+    @pl.when(g == 0)
+    def _():
+        start_own()
+        arrivals(0, 0, chunks)
+        direct(0)
+        arrivals(1, 0, chunks // 2)
+        direct(1)
+        diagonal(0)
+        arrivals(1, chunks // 2, chunks)
+        direct(2)
+        diagonal(1)
+        arrivals(2, 0, txt_chunks)
+        pl.semaphore_signal(go, inc=1, device_id=(1, r, c), device_id_type=MESH)
+
+    @pl.when(g == 1)
+    def _():
+        for p in range(6):
+            direct(p)
+            if p:
+                diagonal(p - 1)
+        diagonal(5)
+        pl.semaphore_wait(go, 1)
+        start_own()
+        arrivals(0, 0, chunks)
+        arrivals(1, 0, chunks)
+        arrivals(2, 0, txt_chunks)
 
     for copy in locals_:
         copy.wait()
     for step in range(1, n_row):
         mods_copy(step).wait_recv()
-
-    @pl.loop(0, chunks)
-    def _(j):
-        for i in range(3):
-            share(j, i).wait_recv()
+    have(0)
+    have(1)
+
+    def passed_on(j):
+        for hops in range(1, last):
+
+            @pl.when((r >= hops) & (r < last))
+            def _():
+                up_copy(hops, j).wait_send()
+
+            @pl.when((r <= last - hops) & (r > 0))
+            def _():
+                dn_copy(hops, j).wait_send()
 
     def normalise(j, first):
+        passed_on(j)
+
         @pl.loop(0, ROWS // 32)
         def _(i):
             parts = []
@@ -315,13 +363,21 @@
             for s in range(n_row):
                 table = mods[pl.ds(s * 16, 16), :].astype(jnp.float32)
                 value = parts[s] * scale * (1.0 + table[first + 1 : first + 2]) + table[first : first + 1]
-                ready[pl.ds(pl.multiple_of(i * 32, 32), 32), pl.ds(s * width, width)] = value.astype(jnp.bfloat16)
-
-    def project(p, put):
+                rows = pl.ds(pl.multiple_of(s * slots + j * ROWS + i * 32, 32), 32)
+                tok[rows, :] = value.astype(jnp.bfloat16)
+
+    def project(p, j, put):
         @pl.loop(0, heads // 2)
         def _(t):
-            block = weights[pl.ds(p * 4 * width, 4 * width), pl.ds(pl.multiple_of(t * 2 * HD, 2 * HD), 2 * HD)]
-            y = jnp.dot(ready[...], block, preferred_element_type=jnp.float32)
+            columns = pl.ds(pl.multiple_of(t * 2 * HD, 2 * HD), 2 * HD)
+            y = sum(
+                jnp.dot(
+                    tok_at(s, j)[...],
+                    weights[pl.ds((p * 4 + s) * width, width), columns],
+                    preferred_element_type=jnp.float32,
+                )
+                for s in range(n_row)
+            )
             put(2 * t, y[:, :HD])
             put(2 * t + 1, y[:, HD:])
 
@@ -341,29 +397,61 @@
 
     @pl.loop(0, txt_chunks)
     def _(j):
-        arrive(2, j)
         normalise(j, 2)
         at = pl.multiple_of(j * ROWS, ROWS)
-        project(0, put_keys(at))
+        project(0, j, put_keys(at))
         place = at + lax.broadcasted_iota(jnp.int32, (ROWS, HD), 0)
-        project(1, put_values(at, jnp.where(place < live_len[0], 1.0, 0.0)))
+        project(1, j, put_values(at, jnp.where(place < live_len[0], 1.0, 0.0)))
 
     q_scale = math.log2(math.e) / math.sqrt(HD)
 
-    @pl.loop(0, img_chunks)
-    def _(i):
-        j = txt_chunks + i
+    def keys(j):
+        project(2, j, put_keys(pl.multiple_of(j * ROWS, ROWS)))
+
+    def values(j):
+        project(3, j, put_values(pl.multiple_of(j * ROWS, ROWS), None))
+
+    def queries(j):
+        row = pl.multiple_of((j - txt_chunks) * ROWS, ROWS)
+
+        def put(h, y):
+            q_buf[h, pl.ds(row, ROWS), :] = (rms_norm(y) * q_scale).astype(jnp.bfloat16)
+
+        project(4, j, put)
+
+    def image_in(j):
         arrive(2, j)
         normalise(j, 0)
-        at = pl.multiple_of(j * ROWS, ROWS)
-        row = pl.multiple_of(i * ROWS, ROWS)
-        project(2, put_keys(at))
-        project(3, put_values(at, None))
-
-        def put_queries(h, y):
-            q_buf[h, pl.ds(row, ROWS), :] = (rms_norm(y) * q_scale).astype(jnp.bfloat16)
-
-        project(4, put_queries)
+
+    def image_rows(*steps):
+        @pl.loop(txt_chunks, chunks)
+        def _(j):
+            for step in steps:
+                step(j)
+
+    @pl.when(g == 0)
+    def _():
+        direct(3)
+        diagonal(2)
+        image_rows(image_in)
+        have(2)
+        image_rows(keys)
+        direct(4)
+        diagonal(3)
+        have(3)
+        image_rows(values)
+        direct(5)
+        diagonal(4)
+        have(4)
+        image_rows(queries)
+        diagonal(5)
+        have(5)
+
+    @pl.when(g == 1)
+    def _():
+        for p in range(2, 6):
+            have(p)
+        image_rows(image_in, keys, values, queries)
 
     @pl.loop(0, 6)
     def _(p):
@@ -423,9 +511,9 @@
     strength = scalars[0]
 
     def finish(b, projected):
-        own = tok[pl.ds(pl.multiple_of(r * slots + texts + b * ROWS, ROWS), ROWS), :].astype(jnp.float32)
+        rows = pl.ds(pl.multiple_of(b * ROWS, ROWS), ROWS)
+        own = out[rows, :].astype(jnp.float32)
         result = (own + gate[...].astype(jnp.float32) * projected).astype(jnp.bfloat16)
-        rows = pl.ds(pl.multiple_of(b * ROWS, ROWS), ROWS)
         out[rows, :] = result
         velocity = jnp.dot(result, final_w[...], preferred_element_type=jnp.float32) * strength
         vel_send[rows, :] = velocity.astype(jnp.bfloat16)
@@ -499,15 +587,13 @@
 
     @pl.loop(0, chunks)
     def _(j):
-        for hops in range(last):
-
-            @pl.when((r >= hops) & (r < last))
-            def _():
-                up_copy(hops, j).wait_send()
-
-            @pl.when((r <= last - hops) & (r > 0))
-            def _():
-                dn_copy(hops, j).wait_send()
+        @pl.when(r < last)
+        def _():
+            up_copy(0, j).wait_send()
+
+        @pl.when(r > 0)
+        def _():
+            dn_copy(0, j).wait_send()
 
     @pl.loop(0, img_chunks)
     def _(b):
@@ -572,7 +658,6 @@
             pltpu.VMEM((4 * slots, width), jnp.bfloat16),
             pltpu.VMEM((24 * width, width), jnp.bfloat16),
             pltpu.VMEM((64, width), jnp.bfloat16),
-            pltpu.VMEM((ROWS, 4 * width), jnp.bfloat16),
             pltpu.VMEM((heads, images, HD), jnp.bfloat16),
             pltpu.VMEM((heads, slots, HD), jnp.bfloat16),
             pltpu.VMEM((heads, slots, 2 * HD), jnp.bfloat16),
@@ -595,7 +680,8 @@
             dma((3, blocks)),
             dma((7,)),
             dma((7,)),
-            dma((9,)),
+            dma((10,)),
+            pltpu.SemaphoreType.REGULAR,
         ],
         compiler_params=pltpu.CompilerParams(
             collective_id=0, has_side_effects=True, vmem_limit_bytes=63 * 1024 * 1024

time: 333 us -> 341 us (1.024)
  Pallas kernels: 310 us -> 318 us
    pallas_call x1, Pallas kernels: 310 us -> 318 us  [fused(): pl.pallas_call(layer_kernel, out_shape=(jax.ShapeDtypeStruct((images, wid...]
where the time goes in v2:
time: 341 us; the launch traced here: 340 us
  Pallas kernels  318 us (93%)
  local copies, waits for them, and re-layouts  17 us (5%)
  between operations  4.09 us (1%)
    pallas_call x1, Pallas kernels, fused(): pl.pallas_call(layer_kernel, out_shape=(jax.ShapeDtypeStruct((images, wid...  318 us
    unnamed x16, local copies, waits for them, and re-layouts  11.6 us

profile of v2, /device:TPU:0, one launch (start us, length us, event | category | flops | bytes accessed | tf_op | source)
XLA Modules:
  0.0 340.1 jit_solution(10442597201694306380)
XLA Ops:
  0.6 0.0 copy-start
  1.4 1.4 fusion.3
  4.8 0.7 pad_maximum_fusion.scalars
  5.5 2.0 copy.16
  7.5 0.0 copy-start.1
  7.5 0.0 copy-start.2
  7.5 0.0 copy-start.3
  7.5 1.6 constant_dynamic-update-slice_fusion.1
  9.1 0.0 copy-done
  9.1 1.1 fusion.2
  10.2 1.1 fusion.1
  11.3 1.1 fusion
  12.4 0.0 copy-done.1
  12.4 1.1 constant_dynamic-update-slice_fusion.own_w
  13.5 1.1 copy.17
  14.6 0.7 pad.4.final_w
  15.3 1.5 copy.18
  16.8 0.1 pad.7.clone
  16.9 0.0 copy-done.2
  16.9 0.0 copy-done.3
  16.9 0.7 maximum_maximum_fusion.mods_hbm
  18.2 317.7 %shard_map.149 = (bf16[1024,768]{1,0:T(8,128)(2,1)}, f32[128,64]{1,0:T(8,128)}) custom-call(f32[2]{0:T(128)} %pad_maximum_fusion.scalars, s32[1]{0:T(128)} %bitcast.27.live_len, bf16[1024,768]{1,0:T(8,128)(2,1)} %bitcast.40, bf16[512,768]{1,0:T(8,128)(2,1)} %bitcast.42, bf16[16,768]{1,0:T(8,128)(2,1)} %maximum_maximum_fusion.mods_hbm, ...), custom_call_target="tpu_custom_call" | custom-call | tf_op jit(solution)/shard_map/pallas_call | solution.py:649
  335.9 1.5 copy.19
  337.4 2.7 copy.28
  (1 shorter events, 0.0 us)
Async XLA Ops:
  0.6 8.4 %copy-start = (bf16[768,3,768]{2,0,1:T(8,128)(2,1)S(1)}, bf16[768,3,768]{2,0,1:T(8,128)(2,1)}, u32[]{:S(2)}) copy-start(bf16[768,3,768]{2,0,1:T(8,128)(2,1)} %param.20) | copy-start | bytes 10616836
  7.5 4.9 %copy-start.1 = (bf16[768,768]{1,0:T(8,128)(2,1)S(1)}, bf16[768,768]{1,0:T(8,128)(2,1)}, u32[]{:S(2)}) copy-start(bf16[768,768]{1,0:T(8,128)(2,1)} %param.22) | copy-start | bytes 3538948
  7.5 9.4 %copy-start.2 = (bf16[1,1,2,768]{3,2,1,0:T(2,128)(2,1)S(1)}, bf16[1,1,2,768]{3,2,1,0:T(2,128)(2,1)}, u32[]{:S(2)}) copy-start(bf16[1,1,2,768]{3,2,1,0:T(2,128)(2,1)} %param.17) | copy-start | bytes 9220
  7.5 9.4 %copy-start.3 = (bf16[1,1,2,768]{3,2,1,0:T(2,128)(2,1)S(1)}, bf16[1,1,2,768]{3,2,1,0:T(2,128)(2,1)}, u32[]{:S(2)}) copy-start(bf16[1,1,2,768]{3,2,1,0:T(2,128)(2,1)} %param.16) | copy-start | bytes 9220
